TPU v7x, 32 devices: a whole 2x2x4 slice. The times are simulated.
32 devices in a mesh: groups: 2 (over y), store: 4 (over z), head: 2 (over x), pair: 2 (over core).
Axes of the slice: x: 2, y: 2, z: 4, core: 2. Of those that a mesh axis runs over, the one named last changes fastest.
Arguments:
- passage_cache: bfloat16 [128, 8, 2, 512, 128], P(('groups', 'store', 'pair'), 'head'), parts along dimension 0, may hold values from -6 to 6
- queries: bfloat16 [16, 32, 24, 64, 128], P(('groups', 'store', 'pair'), None, None, 'head'), parts along dimension 0, may hold values from -64 to 64
- passage_home: int32 [128], P('groups'), parts along dimension 0, may hold values from 0 to 63, as said below
- retrieval: int32 [16, 32], P(('groups', 'store', 'pair')), parts along dimension 0, may hold values from 0 to 63, as said below
- counts: int32 [16], P(('groups', 'store', 'pair')), parts along dimension 0, may hold values from 8 to 32, as said below
- boundary_rows: int32 [16, 32, 24], P(('groups', 'store', 'pair')), parts along dimension 0, may hold values from 0 to 511, as said below
- cross_blocks: int32 [16, 32, 2], P(('groups', 'store', 'pair')), parts along dimension 0, may hold values from 0 to 31, as said below
Outputs:
- attended: bfloat16 [16, 32, 24, 64, 128], P(('groups', 'store', 'pair'), None, None, 'head'), parts along dimension 0
There are 2 independent parts, one for each index of `groups`. A program takes and returns all parts, laid end to end along the dimension named above; each array names one. Nothing has to cross between parts.
Inputs may be any that keep to these rules, and one draw needn't show every extreme that they name: `passage_home`: a permutation: each passage has one row of passage_cache, and rows s * 8 to (s + 1) * 8 - 1 form cache shard s. `retrieval`: the ids of one request are distinct; among its live slots at most 4 lie on one cache shard, and the request with 32 live slots has exactly 4 on every shard; ids in slots from counts[r] on are never read. `counts`: some request has 32 live slots. `boundary_rows`: distinct and rising within one slot. `cross_blocks`: an entry of slot j is an earlier slot or j itself, which stands for no passage; the earlier slots listed for one slot are distinct.
All inputs are finite; a program needn't handle non-finite values.
Results may differ from a plain program's by a relative error of at most 0.0034.
Values may be sent and summed in bfloat16 or wider, within the bound.
A program may use at most 192 MiB of HBM per device.

v0:
```python
import functools

import jax
import jax.numpy as jnp
from jax import lax
from jax.experimental import pallas as pl
from jax.experimental.pallas import tpu as pltpu
from jax.sharding import PartitionSpec as P

VMEM_BYTES = 48 * 1024 * 1024


def blank_kernel(out_ref):
    pass


def blank(shape, dtype):
    return pl.pallas_call(
        blank_kernel,
        out_shape=jax.ShapeDtypeStruct(shape, dtype),
        out_specs=pl.BlockSpec(memory_space=pl.ANY),
    )()


def attend_kernel(br, now, spans, order, place, extra, rows, q_ref, own_ref, one_ref, two_ref, prev_ref, out_ref):
    heads, total_rows, depth = q_ref.shape[1:]
    group = total_rows // br
    length = own_ref.shape[3]
    scale = depth ** (-0.5)
    step = pl.program_id(0)
    base = now[0] * 3
    index = spans[base] + step
    active = step < spans[base + 1]
    slot = order[jnp.minimum(index, order.shape[0] - 1)]
    live = jnp.logical_and(active, index < spans[base + 2])
    links = extra[slot]

    def run(kv_refs):
        position = lax.broadcasted_iota(jnp.int32, (group, length), 1)
        allowed = jnp.concatenate(
            [(position <= rows[slot * br + b]).astype(jnp.int32) for b in range(br)], axis=0
        ) > 0
        for h in range(heads):
            query = q_ref[0, h]
            scores = [
                lax.dot_general(
                    query, ref[0, h, 0], (((1,), (1,)), ((), ())), preferred_element_type=jnp.float32
                )
                for ref in kv_refs
            ]
            scores[0] = jnp.where(allowed, scores[0], -jnp.inf)
            peak = functools.reduce(jnp.maximum, scores)
            peak = jnp.max(peak, axis=1, keepdims=True)
            expon = [jnp.exp((s - peak) * scale) for s in scores]
            totals = jnp.sum(functools.reduce(jnp.add, expon), axis=1, keepdims=True)
            mixed = functools.reduce(
                jnp.add,
                [
                    jnp.dot(e.astype(jnp.bfloat16), ref[0, h, 1], preferred_element_type=jnp.float32)
                    for e, ref in zip(expon, kv_refs)
                ],
            )
            out_ref[0, h] = (mixed / totals).astype(out_ref.dtype)

    @pl.when(jnp.logical_and(live, links == 0))
    def _():
        run([own_ref])

    @pl.when(jnp.logical_and(live, links == 1))
    def _():
        run([own_ref, one_ref])

    @pl.when(jnp.logical_and(live, links == 2))
    def _():
        run([own_ref, one_ref, two_ref])

    @pl.when(jnp.logical_and(active, jnp.logical_not(live)))
    def _():
        out_ref[...] = jnp.zeros_like(out_ref)


def attend(steps, br, now, spans, order, place, extra, rows, q, buf, prev):
    slots, heads, total_rows, depth = q.shape
    kv_block = (1,) + buf.shape[1:]

    def pick(k, now, spans, order):
        base = now[0] * 3
        index = jnp.minimum(spans[base] + jnp.minimum(k, spans[base + 1] - 1), spans[base + 2] - 1)
        return order[jnp.clip(index, 0, slots - 1)]

    def q_map(k, now, spans, order, place, extra, rows):
        return (pick(k, now, spans, order), 0, 0, 0)

    def kv_map(which, k, now, spans, order, place, extra, rows):
        return (place[pick(k, now, spans, order) * 3 + which], 0, 0, 0, 0)

    def out_map(k, now, spans, order, place, extra, rows):
        base = now[0] * 3
        index = jnp.clip(spans[base] + k, 0, slots - 1)
        return (jnp.where(k < spans[base + 1], order[index], slots), 0, 0, 0)

    return pl.pallas_call(
        functools.partial(attend_kernel, br),
        out_shape=jax.ShapeDtypeStruct(prev.shape, prev.dtype),
        grid_spec=pltpu.PrefetchScalarGridSpec(
            num_scalar_prefetch=6,
            grid=(steps,),
            in_specs=[pl.BlockSpec((1, heads, total_rows, depth), q_map)]
            + [pl.BlockSpec(kv_block, functools.partial(kv_map, w)) for w in range(3)]
            + [pl.BlockSpec(memory_space=pl.ANY)],
            out_specs=pl.BlockSpec((1, heads, total_rows, depth), out_map),
        ),
        input_output_aliases={10: 0},
        compiler_params=pltpu.CompilerParams(
            dimension_semantics=("arbitrary",), vmem_limit_bytes=VMEM_BYTES
        ),
        cost_estimate=pl.CostEstimate(
            flops=4 * steps * heads * total_rows * 3 * buf.shape[3] * depth,
            bytes_accessed=steps * 4 * heads * buf.shape[3] * depth * 6,
            transcendentals=steps * heads * total_rows * 3 * buf.shape[3],
        ),
    )(now, spans, order, place, extra, rows, q, buf, buf, buf, prev)


def local(passage_cache, queries, passage_home, retrieval, counts, boundary_rows, cross_blocks):
    slots = retrieval.shape[1]
    br = queries.shape[2]
    kv_heads = passage_cache.shape[1]
    group_size = queries.shape[3] // kv_heads
    depth = queries.shape[4]
    slot_ids = jnp.arange(slots, dtype=jnp.int32)
    live = slot_ids < counts[0]
    places = passage_home[retrieval[0]]

    links = cross_blocks[0]
    valid = links != slot_ids[:, None]
    count_links = jnp.sum(valid.astype(jnp.int32), axis=1)
    first = jnp.where(valid[:, 0], links[:, 0], links[:, 1])
    first = jnp.where(count_links >= 1, first, slot_ids)
    second = jnp.where(count_links >= 2, links[:, 1], first)
    members = jnp.stack([slot_ids, first, second], axis=1)
    member_hit = (members[:, :, None] == slot_ids[None, None, :]) & live[None, None, :]
    place = jnp.sum(jnp.where(member_hit, places[None, None, :], 0), axis=2).reshape(-1)
    rows = boundary_rows[0].reshape(-1)
    now = jnp.zeros((1,), jnp.int32)
    spans = jnp.stack([jnp.int32(0), jnp.int32(slots), counts[0]])

    cuts = [(0, kv_heads - 1), (kv_heads - 1, kv_heads)] if kv_heads > 1 else [(0, kv_heads)]
    q = queries[0].reshape(slots, br, kv_heads, group_size, depth)
    parts = []
    gathered = None
    for low, high in cuts:
        piece = passage_cache[:, low:high]
        if gathered is not None:
            piece, gathered = lax.optimization_barrier((piece, gathered))
            parts.append((gathered,) + parts.pop()[1:])
        gathered = lax.all_gather(piece, ("store", "pair"), axis=0, tiled=True)
        q_part = jnp.transpose(q[:, :, low:high], (0, 2, 1, 3, 4))
        parts.append((gathered, q_part.reshape(slots, high - low, br * group_size, depth)))
    outs = []
    for kv, q_part in parts:
        out = blank((slots + 1,) + q_part.shape[1:], q.dtype)
        out = attend(slots, br, now, spans, slot_ids, place, count_links, rows, q_part, kv, out)
        out = out[:slots].reshape(slots, q_part.shape[1], br, group_size, depth)
        outs.append(jnp.transpose(out, (0, 2, 1, 3, 4)))
    return jnp.concatenate(outs, axis=2).reshape(queries.shape)


def solution(mesh):
    return jax.shard_map(
        local,
        mesh=mesh,
        in_specs=(
            P(("groups", "store", "pair"), "head", None, None, None),
            P(("groups", "store", "pair"), None, None, "head", None),
            P("groups"),
            P(("groups", "store", "pair"), None),
            P(("groups", "store", "pair")),
            P(("groups", "store", "pair"), None, None),
            P(("groups", "store", "pair"), None, None),
        ),
        out_specs=P(("groups", "store", "pair"), None, None, "head", None),
        check_vma=False,
    )
```

profile of v0, /device:TPU:5, one launch (start us, length us, event | category | flops | bytes accessed | tf_op | source)
XLA Modules:
  0.0 635.7 jit_solution(5748105892242572224)
XLA Ops:
  6.5 0.0 copy-start
  6.5 6.2 slice.33
  12.7 0.0 all-gather.3.cloned.1.call-update
  12.8 0.0 all-gather.5.cloned.1.call-start
  12.8 3.1 slice.32
  15.9 426.0 %all-gather.3.cloned.1.call-done.own_ref.one_ref.two_ref = bf16[64,3,2,512,128]{4,3,2,1,0:T(8,128)(2,1)} async-done(((bf16[8,3,2,512,128]{4,3,2,1,0:T(8,128)(2,1)}), bf16[64,3,2,512,128]{4,3,2,1,0:T(8,128)(2,1)}) %all-gather.3.cloned.1.call-update) | async-done | bytes 50331664 | tf_op jit(solution)/shard_map/all_gather | solution.py:157
  442.0 0.0 all-gather.5.cloned.1.call-update
  442.7 0.7 gather_fusion
  443.4 0.0 copy-done.5
  443.5 0.2 select_reduce_fusion
  443.7 0.1 copy.27
  443.8 0.1 reshape.66.place
  443.9 0.1 copy.28
  444.0 0.1 reshape_squeeze.6.rows
  444.1 0.1 pad_add_fusion.1.spans
  444.1 1.5 slice_bitcast_fusion.2.q_ref
  445.7 3.5 copy_bitcast_fusion.1.q_ref
  449.2 62.3 %shard_map.74 = bf16[33,3,192,128]{3,2,1,0:T(8,128)(2,1)} custom-call(s32[1]{0:T(128)} %constant.6.clone.1.now, s32[3]{0:T(128)S(1)} %pad_add_fusion.1.spans, s32[32]{0:T(128)S(1)} %iota.21.order, s32[96]{0:T(128)S(1)} %reshape.66.place, s32[32]{0:T(128)S(1)} %get-tuple-element.11.extra, ...), custom_call_target="tpu_custom_call", output_to_operand_aliasing={{}: (10, {})} | custom-call | flops 14495514624 | bytes 150994944 | tf_op jit(solution)/shard_map/pallas_call | solution.py:102
  511.5 5.0 slice_bitcast_fusion
  516.5 76.4 %all-gather.5.cloned.1.call-done.own_ref.one_ref.two_ref = bf16[64,1,2,512,128]{4,3,2,1,0:T(8,128)(2,1)} async-done(((bf16[8,1,2,512,128]{4,3,2,1,0:T(8,128)(2,1)}), bf16[64,1,2,512,128]{4,3,2,1,0:T(8,128)(2,1)}) %all-gather.5.cloned.1.call-update) | async-done | bytes 16777232 | tf_op jit(solution)/shard_map/all_gather | solution.py:157
  592.9 32.4 %shard_map.76 = bf16[33,1,192,128]{3,2,1,0:T(8,128)(2,1)S(1)} custom-call(s32[1]{0:T(128)} %constant.6.clone.1.now, s32[3]{0:T(128)S(1)} %pad_add_fusion.1.spans, s32[32]{0:T(128)S(1)} %iota.25.order, s32[96]{0:T(128)S(1)} %reshape.66.place, s32[32]{0:T(128)S(1)} %get-tuple-element.11.extra, ...), custom_call_target="tpu_custom_call", output_to_operand_aliasing={{}: (10, {})} | custom-call | flops 4831838208 | bytes 50331648 | tf_op jit(solution)/shard_map/pallas_call | solution.py:102
  625.3 0.0 copy-start.1
  625.3 0.1 slice_bitcast_fusion.1
  625.4 3.4 copy_bitcast_fusion
  (23 shorter events, 0.1 us)
Async XLA Ops:
  6.5 436.1 %copy-start = (s32[64]{0:T(128)S(1)}, s32[64]{0:T(128)}, u32[]{:S(2)}) copy-start(s32[64]{0:T(128)} %param.9) | copy-start | bytes 772
  6.5 435.4 %all-gather.3.cloned.1.call-start = ((), (), s32[]{:S(2)}) async-start(), calls=%async_computation | async-start | bytes 56623104 | tf_op jit(solution)/shard_map/all_gather | solution.py:157
  12.8 580.1 %all-gather.5.cloned.1.call-start = ((), (), s32[]{:S(2)}) async-start(), calls=%async_computation.1 | async-start | bytes 18874368 | tf_op jit(solution)/shard_map/all_gather | solution.py:157
  15.9 426.7 %copy-start.6 = (s32[1,32]{1,0:T(1,128)S(1)}, s32[1,32]{1,0:T(1,128)}, u32[]{:S(2)}) copy-start(s32[1,32]{1,0:T(1,128)} %param.10) | copy-start | bytes 388
  15.9 427.5 %copy-start.5 = (s32[1,32,2]{1,2,0:T(2,128)S(1)}, s32[1,32,2]{1,2,0:T(2,128)}, u32[]{:S(2)}) copy-start(s32[1,32,2]{1,2,0:T(2,128)} %param.13) | copy-start | bytes 772
  15.9 427.9 %copy-start.4 = (s32[1,32,24]{1,2,0:T(8,128)S(1)}, s32[1,32,24]{1,2,0:T(8,128)}, u32[]{:S(2)}) copy-start(s32[1,32,24]{1,2,0:T(8,128)} %param.12) | copy-start | bytes 9220
  511.5 81.4 %copy-start.2 = (bf16[33,1,192,128]{3,2,1,0:T(8,128)(2,1)S(1)}, bf16[33,1,192,128]{3,2,1,0:T(8,128)(2,1)}, u32[]{:S(2)}) copy-start(bf16[33,1,192,128]{3,2,1,0:T(8,128)(2,1)} %shard_map.75.prev_ref) | copy-start | bytes 4866052
  592.9 32.5 %copy-start.3 = (bf16[32,24,3,8,128]{4,3,1,2,0:T(8,128)(2,1)S(1)}, bf16[32,24,3,8,128]{4,3,1,2,0:T(8,128)(2,1)}, u32[]{:S(2)}) copy-start(bf16[32,24,3,8,128]{4,3,1,2,0:T(8,128)(2,1)} %slice_bitcast_fusion) | copy-start | bytes 14155780
  625.3 3.5 copy-start.1
Sparse Core Ops, SparseCore 0:
  12.9 429.0 all-gather.2
  443.5 149.2 all-gather.4
where the time goes:
time: 636 us
  waiting for transfers between devices  502 us (79%)
  Pallas kernels  94.7 us (15%)
  local copies, waits for them, and re-layouts  20.6 us (3%)
  between operations  14.2 us (2%)
    all_gather x2, waiting for transfers between devices, local(): gathered = lax.all_gather(piece, ('store', 'pair'), axis=0, tiled=True)  502 us
    pallas_call x2, Pallas kernels, attend(): pl.pallas_call(functools.partial(attend_kernel, br), out_shape=jax.ShapeD...  94.7 us
  transfers between devices with their start and end apart: 2, of which 2 were waited for; matrix products, arithmetic and copies ran while one was open for 2% of the time, Pallas kernels for 10%

commit v1 on v0

--- a/solution.py
+++ b/solution.py
@@ -40,15 +40,18 @@
         allowed = jnp.concatenate(
             [(position <= rows[slot * br + b]).astype(jnp.int32) for b in range(br)], axis=0
         ) > 0
-        for h in range(heads):
-            query = q_ref[0, h]
+        cuts = 2 if heads == 1 and total_rows % 32 == 0 else 1
+        part = total_rows // cuts
+        for h, c in [(h, c) for h in range(heads) for c in range(cuts)]:
+            span_rows = slice(c * part, (c + 1) * part)
+            query = q_ref[0, h, span_rows]
             scores = [
                 lax.dot_general(
                     query, ref[0, h, 0], (((1,), (1,)), ((), ())), preferred_element_type=jnp.float32
                 )
                 for ref in kv_refs
             ]
-            scores[0] = jnp.where(allowed, scores[0], -jnp.inf)
+            scores[0] = jnp.where(allowed[span_rows], scores[0], -jnp.inf)
             peak = functools.reduce(jnp.maximum, scores)
             peak = jnp.max(peak, axis=1, keepdims=True)
             expon = [jnp.exp((s - peak) * scale) for s in scores]
@@ -60,7 +63,7 @@
                     for e, ref in zip(expon, kv_refs)
                 ],
             )
-            out_ref[0, h] = (mixed / totals).astype(out_ref.dtype)
+            out_ref[0, h, span_rows] = (mixed / totals).astype(out_ref.dtype)
 
     @pl.when(jnp.logical_and(live, links == 0))
     def _():

time: 636 us -> 640 us (level)
  no operation moved by 1% of the time
where the time goes in v1:
time: 640 us
  waiting for transfers between devices  502 us (78%)
  Pallas kernels  99.3 us (16%)
  local copies, waits for them, and re-layouts  20.6 us (3%)
  between operations  14.2 us (2%)
    all_gather x2, waiting for transfers between devices, local(): gathered = lax.all_gather(piece, ('store', 'pair'), axis=0, tiled=True)  502 us
    pallas_call x2, Pallas kernels, attend(): pl.pallas_call(functools.partial(attend_kernel, br), out_shape=jax.ShapeD...  99.3 us
  transfers between devices with their start and end apart: 2, of which 2 were waited for; matrix products, arithmetic and copies ran while one was open for 2% of the time, Pallas kernels for 10%

profile of v1, /device:TPU:5, one launch (start us, length us, event | category | flops | bytes accessed | tf_op | source)
XLA Modules:
  0.0 640.0 jit_solution(13904689580247773404)
XLA Ops:
  6.5 0.0 copy-start
  6.5 6.2 slice.33
  12.7 0.0 all-gather.3.cloned.1.call-update
  12.8 0.0 all-gather.5.cloned.1.call-start
  12.8 3.1 slice.32
  15.9 426.0 %all-gather.3.cloned.1.call-done.own_ref.one_ref.two_ref = bf16[64,3,2,512,128]{4,3,2,1,0:T(8,128)(2,1)} async-done(((bf16[8,3,2,512,128]{4,3,2,1,0:T(8,128)(2,1)}), bf16[64,3,2,512,128]{4,3,2,1,0:T(8,128)(2,1)}) %all-gather.3.cloned.1.call-update) | async-done | bytes 50331664 | tf_op jit(solution)/shard_map/all_gather | solution.py:160
  442.0 0.0 all-gather.5.cloned.1.call-update
  442.7 0.0 copy-done
  442.7 0.7 gather_fusion
  443.5 0.2 select_reduce_fusion
  443.7 0.1 copy.27
  443.8 0.1 reshape.66.place
  443.9 0.1 copy.28
  444.0 0.1 reshape_squeeze.6.rows
  444.1 0.1 pad_add_fusion.1.spans
  444.1 1.5 slice_bitcast_fusion.2.q_ref
  445.7 3.5 copy_bitcast_fusion.1.q_ref
  449.2 62.6 %shard_map.74 = bf16[33,3,192,128]{3,2,1,0:T(8,128)(2,1)} custom-call(s32[1]{0:T(128)} %constant.6.clone.1.now, s32[3]{0:T(128)S(1)} %pad_add_fusion.1.spans, s32[32]{0:T(128)S(1)} %iota.21.order, s32[96]{0:T(128)S(1)} %reshape.66.place, s32[32]{0:T(128)S(1)} %get-tuple-element.11.extra, ...), custom_call_target="tpu_custom_call", output_to_operand_aliasing={{}: (10, {})} | custom-call | flops 14495514624 | bytes 150994944 | tf_op jit(solution)/shard_map/pallas_call | solution.py:105
  511.8 5.0 slice_bitcast_fusion
  516.8 76.1 %all-gather.5.cloned.1.call-done.own_ref.one_ref.two_ref = bf16[64,1,2,512,128]{4,3,2,1,0:T(8,128)(2,1)} async-done(((bf16[8,1,2,512,128]{4,3,2,1,0:T(8,128)(2,1)}), bf16[64,1,2,512,128]{4,3,2,1,0:T(8,128)(2,1)}) %all-gather.5.cloned.1.call-update) | async-done | bytes 16777232 | tf_op jit(solution)/shard_map/all_gather | solution.py:160
  592.9 36.7 %shard_map.76 = bf16[33,1,192,128]{3,2,1,0:T(8,128)(2,1)S(1)} custom-call(s32[1]{0:T(128)} %constant.6.clone.1.now, s32[3]{0:T(128)S(1)} %pad_add_fusion.1.spans, s32[32]{0:T(128)S(1)} %iota.25.order, s32[96]{0:T(128)S(1)} %reshape.66.place, s32[32]{0:T(128)S(1)} %get-tuple-element.11.extra, ...), custom_call_target="tpu_custom_call", output_to_operand_aliasing={{}: (10, {})} | custom-call | flops 4831838208 | bytes 50331648 | tf_op jit(solution)/shard_map/pallas_call | solution.py:105
  629.6 0.0 copy-start.1
  629.6 0.1 slice_bitcast_fusion.1
  629.7 3.4 copy_bitcast_fusion
  (23 shorter events, 0.1 us)
Async XLA Ops:
  6.5 436.1 %copy-start = (s32[64]{0:T(128)S(1)}, s32[64]{0:T(128)}, u32[]{:S(2)}) copy-start(s32[64]{0:T(128)} %param.9) | copy-start | bytes 772
  6.5 435.4 %all-gather.3.cloned.1.call-start = ((), (), s32[]{:S(2)}) async-start(), calls=%async_computation | async-start | bytes 56623104 | tf_op jit(solution)/shard_map/all_gather | solution.py:160
  12.8 580.1 %all-gather.5.cloned.1.call-start = ((), (), s32[]{:S(2)}) async-start(), calls=%async_computation.1 | async-start | bytes 18874368 | tf_op jit(solution)/shard_map/all_gather | solution.py:160
  15.9 426.7 %copy-start.6 = (s32[1,32]{1,0:T(1,128)S(1)}, s32[1,32]{1,0:T(1,128)}, u32[]{:S(2)}) copy-start(s32[1,32]{1,0:T(1,128)} %param.10) | copy-start | bytes 388
  15.9 427.5 %copy-start.5 = (s32[1,32,2]{1,2,0:T(2,128)S(1)}, s32[1,32,2]{1,2,0:T(2,128)}, u32[]{:S(2)}) copy-start(s32[1,32,2]{1,2,0:T(2,128)} %param.13) | copy-start | bytes 772
  15.9 427.9 %copy-start.4 = (s32[1,32,24]{1,2,0:T(8,128)S(1)}, s32[1,32,24]{1,2,0:T(8,128)}, u32[]{:S(2)}) copy-start(s32[1,32,24]{1,2,0:T(8,128)} %param.12) | copy-start | bytes 9220
  511.8 81.1 %copy-start.2 = (bf16[33,1,192,128]{3,2,1,0:T(8,128)(2,1)S(1)}, bf16[33,1,192,128]{3,2,1,0:T(8,128)(2,1)}, u32[]{:S(2)}) copy-start(bf16[33,1,192,128]{3,2,1,0:T(8,128)(2,1)} %shard_map.75.prev_ref) | copy-start | bytes 4866052
  592.9 36.8 %copy-start.3 = (bf16[32,24,3,8,128]{4,3,1,2,0:T(8,128)(2,1)S(1)}, bf16[32,24,3,8,128]{4,3,1,2,0:T(8,128)(2,1)}, u32[]{:S(2)}) copy-start(bf16[32,24,3,8,128]{4,3,1,2,0:T(8,128)(2,1)} %slice_bitcast_fusion) | copy-start | bytes 14155780
  629.6 3.5 copy-start.1
Sparse Core Ops, SparseCore 0:
  12.9 429.0 all-gather.2
  443.5 149.2 all-gather.4
